TPU v7x, 32 devices: a whole 2x2x4 slice. The times are simulated.
32 devices in a mesh: pole: 4 (over x, core), grid: 8 (over z, y).
Axes of the slice: x: 2, y: 2, z: 4, core: 2. Of those that a mesh axis runs over, the one named last changes fastest.
Arguments:
- trailing: bfloat16 [4, 2, 4096, 4096], P('pole', None, 'grid'), may hold values from -4.5 to 4.5, as said below
- panel: bfloat16 [4, 2, 4096, 256], P('pole', None, 'grid'), may hold values from -0.0625 to 0.0625
- diag_inverse: bfloat16 [4, 2, 256, 256], P('pole', None, 'grid'), may hold values from -6 to 6
- pole_weights: float32 [4, 2], P('pole'), may hold values from -3 to 3
- owner_map: int32 [4096, 1], P('grid'), may hold values from 0 to 3; in each aligned block of 512 rows (0 to 511, 512 to 1023, ...) at most 256 rows name the same one
- ham_slab: bfloat16 [256, 4096], replicated, may hold values from -0.375 to 0.375
Outputs:
- density_diag: float32 [256, 256], P('grid')
- patch_energy: bfloat16 [8192, 4096], P(('pole', 'grid'))
Inputs may be any that keep to these rules, and one draw needn't show every extreme that they name: trailing is symmetric in its last two dimensions: trailing[p, c, i, j] = trailing[p, c, j, i]. `owner_map`: in each aligned block of 512 rows (the rows of one index of grid) at most 256 rows name the same owner, and some block reaches 256.
All inputs are finite; a program needn't handle non-finite values.
Results may differ from a plain program's by a relative error of at most 0.011.
Values may be sent and summed in bfloat16 or wider, within the bound.
A program may use at most 64 MiB of HBM per device.

v0:
```python
import jax
import jax.numpy as jnp
from jax import lax
from jax.sharding import PartitionSpec as P


def complex_product(left_real, left_imag, right_real, right_imag, form):

    def product(first, second):
        return jnp.einsum(form, first, second, preferred_element_type=jnp.float32)

    real = product(left_real, right_real) - product(left_imag, right_imag)
    imag = product(left_real, right_imag) + product(left_imag, right_real)
    return (real, imag)


def per_device(trailing, panel, diag_inverse, pole_weights, owner_map, ham_slab):
    rows_here = trailing.shape[2]
    piece = lax.all_gather(panel, "grid", axis=2, tiled=True)
    real, imag = complex_product(
        trailing[:, 0], trailing[:, 1], piece[:, 0], piece[:, 1], "prn,pnw->prw"
    )
    cross_real = (-real).astype(jnp.bfloat16)
    cross_imag = (-imag).astype(jnp.bfloat16)
    weight_real = pole_weights[:, 0][:, None, None]
    weight_imag = pole_weights[:, 1][:, None, None]
    density_rows = jnp.sum(
        weight_real * cross_imag.astype(jnp.float32) + weight_imag * cross_real.astype(jnp.float32),
        axis=0,
    )
    quad_real, quad_imag = complex_product(
        panel[:, 0], panel[:, 1], cross_real, cross_imag, "prw,prv->pwv"
    )
    quad_part = -jnp.sum(weight_real * quad_imag + weight_imag * quad_real, axis=0)
    diag_term = jnp.sum(
        weight_real * diag_inverse[:, 1].astype(jnp.float32)
        + weight_imag * diag_inverse[:, 0].astype(jnp.float32),
        axis=0,
    )
    mine = lax.psum_scatter(quad_part, "grid", scatter_dimension=0, tiled=True) + diag_term
    density_diag = lax.psum(mine, "pole")
    owners = owner_map[:, 0]
    capacity = 2 * rows_here // lax.axis_size("pole")
    same = owners[:, None] == owners[None, :]
    earlier = lax.broadcasted_iota(jnp.int32, (rows_here, rows_here), 1) < lax.broadcasted_iota(
        jnp.int32, (rows_here, rows_here), 0
    )
    rank = jnp.sum((same & earlier).astype(jnp.int32), axis=1)
    slot = owners * capacity + rank
    all_slots = lax.axis_size("pole") * capacity
    placement = (
        slot[:, None] == lax.broadcasted_iota(jnp.int32, (rows_here, all_slots), 1)
    ).astype(jnp.float32)
    total_rows = lax.psum(density_rows, "pole")
    chosen = lax.dynamic_slice_in_dim(placement, lax.axis_index("pole") * capacity, capacity, 1)
    owned_rows = jnp.einsum("rs,rw->sw", chosen, total_rows, precision=lax.Precision.HIGHEST)
    patch = owned_rows.astype(jnp.bfloat16)
    patch_energy = jnp.dot(patch, ham_slab, preferred_element_type=jnp.float32).astype(jnp.bfloat16)
    return (density_diag, patch_energy)


def solution(mesh):
    placed = (
        P("pole", None, "grid", None),
        P("pole", None, "grid", None),
        P("pole", None, "grid", None),
        P("pole", None),
        P("grid", None),
        P(),
    )
    return jax.shard_map(
        per_device,
        mesh=mesh,
        in_specs=placed,
        out_specs=(P("grid", None), P(("pole", "grid"), None)),
        check_vma=False,
    )
```

profile of v0, /device:TPU:0, one launch (start us, length us, event | category | flops | bytes accessed | tf_op | source)
XLA Modules:
  0.0 217.7 jit_solution(6838420426173533907)
XLA Ops:
  7.2 0.0 copy-start
  7.2 0.0 all-gather.2.cloned.1.call-start
  7.2 0.7 all-gather.2.cloned.1.call-update
  7.9 0.0 all-reduce.2.cloned.1.call-start
  8.0 0.7 fusion.48
  8.7 0.1 copy.19
  8.8 0.1 copy.20
  8.9 1.4 fusion.49
  10.3 1.0 convert_reduce_fusion
  11.3 0.7 multiply_add_fusion.1
  12.0 74.3 %all-gather.2.cloned.1.call-done = bf16[1,2,4096,256]{3,2,1,0:T(8,128)(2,1)} async-done(((bf16[1,2,512,256]{3,2,1,0:T(8,128)(2,1)}), bf16[1,2,4096,256]{3,2,1,0:T(8,128)(2,1)}) %all-gather.2.cloned.1.call-update) | async-done | bytes 4194320 | tf_op jit(solution)/shard_map/all_gather | solution.py:19
  86.3 4.2 %fusion.2 = f32[512,256]{1,0:T(8,128)S(1)} fusion(bf16[1,2,512,4096]{3,2,1,0:T(8,128)(2,1)} %param.6, bf16[1,2,4096,256]{3,2,1,0:T(8,128)(2,1)} %all-gather.2.cloned.1.call-done), kind=kOutput, calls=%fused_computation.3 | convolution fusion | flops 1073741824 | bytes 6815744 | tf_op jit(solution)/shard_map/prn,pnw->prw/dot_general | solution.py:10
  90.6 1.0 copy-done.2
  91.6 3.0 %fusion = f32[512,256]{1,0:T(8,128)S(1)} fusion(bf16[1,2,512,4096]{3,2,1,0:T(8,128)(2,1)S(1)} %copy-done.2, bf16[1,2,4096,256]{3,2,1,0:T(8,128)(2,1)} %all-gather.2.cloned.1.call-done), kind=kOutput, calls=%fused_computation.1 | convolution fusion | flops 1073741824 | bytes 6815744 | tf_op jit(solution)/shard_map/prn,pnw->prw/dot_general | solution.py:10
  94.6 1.3 fusion.27
  95.9 3.4 %multiply_add_fusion = (f32[512,256]{1,0:T(8,128)}, bf16[512,256]{1,0:T(8,128)(2,1)S(1)}) fusion(bf16[512,256]{1,0:T(8,128)(2,1)S(1)} %fusion.27, f32[]{:T(128)} %bitcast.7, f32[]{:T(128)} %bitcast, f32[512,256]{1,0:T(8,128)S(1)} %fusion, bf16[1,2,4096,256]{3,2,1,0:T(8,128)(2,1)S(1)} %copy-done.3, bf16[1,2,512,4096]{3,2,1,0:T(8,128)(2,1)S(1)} %copy-done.2), kind=kOutput, calls=%fused_computation.33 | convolution fusion | flops 1074790400 | bytes 7864328 | tf_op jit(solution)/shard_map/prn,pnw->prw/dot_general | solution.py:10
  99.3 0.3 fusion.40
  99.6 0.9 fusion.30
  100.5 0.0 all-reduce.2.cloned.1.call-update
  100.5 0.0 reduce-scatter.4.cloned.1.call-start
  100.6 0.3 fusion.42
  100.9 0.9 fusion.34
  101.8 0.8 copy.17
  102.6 0.0 reduce-scatter.4.cloned.1.call-update
  102.6 29.5 %all-reduce.2.cloned.1.call-done = f32[512,256]{1,0:T(8,128)} async-done(((f32[512,256]{1,0:T(8,128)}), f32[512,256]{1,0:T(8,128)}) %all-reduce.2.cloned.1.call-update) | async-done | bytes 524304 | tf_op jit(solution)/shard_map/psum | solution.py:54
  132.1 1.7 convolution_convert_fusion.1
  133.9 2.0 convolution_convert_fusion
  135.9 60.9 %reduce-scatter.4.cloned.1.call-done = f32[32,256]{1,0:T(8,128)} async-done(((f32[256,256]{1,0:T(8,128)}), f32[32,256]{1,0:T(8,128)}) %reduce-scatter.4.cloned.1.call-update) | async-done | bytes 32784
  196.8 0.9 copy.18
  197.6 1.4 bitcast_add_fusion
  199.0 11.5 %psum.14 = f32[32,256]{0,1:T(8,128)S(1)} all-reduce(f32[32,256]{0,1:T(8,128)S(1)} %bitcast_add_fusion), channel_id=1, replica_groups=mesh['pole'=4,'grid'=8] {'pole'}, use_global_device_ids=true, to_apply=%region_1.0 | all-reduce | flops 8192 | bytes 65536 | tf_op jit(solution)/shard_map/psum | solution.py:41
  210.5 0.7 copy.16
  (6 shorter events, 0.0 us)
Async XLA Ops:
  7.2 126.7 %copy-start = (bf16[256,4096]{1,0:T(8,128)(2,1)S(1)}, bf16[256,4096]{1,0:T(8,128)(2,1)}, u32[]{:S(2)}) copy-start(bf16[256,4096]{1,0:T(8,128)(2,1)} %param.11) | copy-start | bytes 6291460
  7.2 79.1 %all-gather.2.cloned.1.call-start = ((), (), s32[]{:S(2)}) async-start(), calls=%async_computation.1 | async-start | bytes 4718592 | tf_op jit(solution)/shard_map/all_gather | solution.py:19
  7.9 124.2 %all-reduce.2.cloned.1.call-start = ((), (), s32[]{:S(2)}) async-start(), calls=%async_computation.2 | async-start | bytes 1048576 | tf_op jit(solution)/shard_map/psum | solution.py:54
  86.3 5.2 %copy-start.2 = (bf16[1,2,512,4096]{3,2,1,0:T(8,128)(2,1)S(1)}, bf16[1,2,512,4096]{3,2,1,0:T(8,128)(2,1)}, u32[]{:S(2)}) copy-start(bf16[1,2,512,4096]{3,2,1,0:T(8,128)(2,1)} %param.6) | copy-start | bytes 25165828
  91.6 3.0 %copy-start.3 = (bf16[1,2,4096,256]{3,2,1,0:T(8,128)(2,1)S(1)}, bf16[1,2,4096,256]{3,2,1,0:T(8,128)(2,1)}, u32[]{:S(2)}) copy-start(bf16[1,2,4096,256]{3,2,1,0:T(8,128)(2,1)} %all-gather.2.cloned.1.call-done) | copy-start | bytes 12582916
  95.8 3.4 %copy-start.1 = (bf16[1,2,512,256]{3,2,1,0:T(8,128)(2,1)S(1)}, bf16[1,2,512,256]{3,2,1,0:T(8,128)(2,1)}, u32[]{:S(2)}) copy-start(bf16[1,2,512,256]{3,2,1,0:T(8,128)(2,1)} %param.7) | copy-start | bytes 1572868
  100.5 96.2 %reduce-scatter.4.cloned.1.call-start = ((), (), s32[]{:S(2)}) async-start(), calls=%async_computation.3 | async-start | bytes 294912
Sparse Core Ops, SparseCore 0:
  10.2 76.0 all-gather.1
  100.7 31.4 all-reduce.1
  135.5 61.2 reduce-scatter.3
where the time goes:
time: 218 us
  waiting for transfers between devices  165 us (76%)
  matrix products  18.1 us (8%)
  between operations  13.9 us (6%)
  blocking collectives  11.5 us (5%)
  local copies, waits for them, and re-layouts  5.74 us (3%)
  other arithmetic  3.05 us (1%)
    all_gather x1, waiting for transfers between devices, per_device(): piece = lax.all_gather(panel, 'grid', axis=2, tiled=True)  74.3 us
    unnamed x4, waiting for transfers between devices  61.6 us
    psum x1, waiting for transfers between devices, per_device(): total_rows = lax.psum(density_rows, 'pole')  29.5 us
    dot_general x8, matrix products, product(): return jnp.einsum(form, first, second, preferred_element_type=jnp.float32)  14.3 us
    psum x1, blocking collectives, per_device(): density_diag = lax.psum(mine, 'pole')  11.5 us
  transfers between devices with their start and end apart: 3, of which 3 were waited for; matrix products, arithmetic and copies ran while one was open for 5% of the time, Pallas kernels for 0%

commit v1 on v0

--- a/solution.py
+++ b/solution.py
@@ -1,7 +1,14 @@
+import functools
+
 import jax
 import jax.numpy as jnp
 from jax import lax
+from jax.experimental import pallas as pl
+from jax.experimental.pallas import tpu as pltpu
 from jax.sharding import PartitionSpec as P
+
+MESH = pl.DeviceIdType.MESH
+LAG = 2
 
 
 def complex_product(left_real, left_imag, right_real, right_imag, form):
@@ -14,7 +21,7 @@
     return (real, imag)
 
 
-def per_device(trailing, panel, diag_inverse, pole_weights, owner_map, ham_slab):
+def per_device_small(trailing, panel, diag_inverse, pole_weights, owner_map, ham_slab):
     rows_here = trailing.shape[2]
     piece = lax.all_gather(panel, "grid", axis=2, tiled=True)
     real, imag = complex_product(
@@ -59,7 +66,284 @@
     return (density_diag, patch_energy)
 
 
+def dot(first, second, over_first=1):
+    return lax.dot_general(
+        first, second, (((over_first,), (0,)), ((), ())), preferred_element_type=jnp.float32
+    )
+
+
+def kernel(
+    n_pole, n_grid, trailing, panel, weights, owners, diag, patch_ref, dd_ref,
+    gbuf, lbuf, acc, place, packed, rbuf, qbuf, abuf, sbuf, bbuf, obuf,
+    gsem, lsem, fwd_send, fwd_recv, p_send, p_recv, a_send, a_recv, b_send, b_recv, c_send, c_recv,
+):
+    ny = 2
+    nz = n_grid // ny
+    rows = gbuf.shape[1]
+    half = rows // 2
+    cap = rbuf.shape[1]
+    sub = obuf.shape[1]
+    pole, me = lax.axis_index("pole"), lax.axis_index("grid")
+    z, y = me // ny, me % ny
+
+    gcopies = [
+        pltpu.make_async_copy(trailing.at[0, c], gbuf.at[c], gsem.at[c]) for c in range(2)
+    ]
+    lcopies = [
+        pltpu.make_async_copy(
+            panel.at[0, c, pl.ds(h * half, half)], lbuf.at[me, h, c], lsem.at[2 * h + c]
+        )
+        for h in range(2)
+        for c in range(2)
+    ]
+    for copy in lcopies + gcopies:
+        copy.start()
+
+    barrier = pltpu.get_barrier_semaphore()
+    for k in range(1, n_grid):
+        pl.semaphore_signal(
+            barrier, inc=1, device_id=(pole, lax.rem(me + k, n_grid)), device_id_type=MESH
+        )
+    for k in range(1, n_pole):
+        pl.semaphore_signal(
+            barrier, inc=1, device_id=(lax.rem(pole + k, n_pole), me), device_id_type=MESH
+        )
+
+    names = lax.broadcasted_iota(jnp.int32, (16, rows), 0) == owners[...]
+    ones = names.astype(jnp.float32)
+    before = (
+        lax.broadcasted_iota(jnp.int32, (rows, rows), 0)
+        < lax.broadcasted_iota(jnp.int32, (rows, rows), 1)
+    ).astype(jnp.float32)
+    counts = dot(ones.astype(jnp.bfloat16), before.astype(jnp.bfloat16))
+    rank = jnp.sum(ones * counts, axis=0, keepdims=True).astype(jnp.int32)
+    slot = owners[...] * cap + rank
+    for q in range(n_pole):
+        here = lax.broadcasted_iota(jnp.int32, (cap, rows), 0) + q * cap == slot
+        place[q] = here.astype(jnp.float32).astype(jnp.bfloat16)
+    acc[...] = jnp.zeros_like(acc)
+
+    for copy in lcopies:
+        copy.wait()
+    pl.semaphore_wait(barrier, n_grid - 1 + n_pole - 1)
+
+    def sends(kind, d, h, s, src):
+        own_line = kind == 0
+        first = d == 0
+        turn = (kind == 1) & first & (h == 0)
+        up = (z + 1 < nz) & ((own_line & (first | (s == -1))) | turn)
+        down = (z >= 1) & ((own_line & (first | (s == 1))) | turn)
+        over = own_line & jnp.logical_not((d == 1) & (h == 0))
+        targets = (jnp.minimum(z + 1, nz - 1) * ny + y, jnp.maximum(z - 1, 0) * ny + y, z * ny + 1 - y)
+        out = []
+        for j, (cond, target) in enumerate(zip((up, down, over), targets)):
+            out.append((cond, pltpu.make_async_remote_copy(
+                src_ref=lbuf.at[src, h],
+                dst_ref=lbuf.at[src, h],
+                send_sem=fwd_send.at[(src * 2 + h) * 3 + j],
+                recv_sem=fwd_recv.at[src * 2 + h],
+                device_id=(pole, target),
+                device_id_type=MESH,
+            )))
+        return out
+
+    def event(i):
+        t, r = i // 4, i % 4
+        kind, side = r // 2, r % 2
+        tt = jnp.maximum(t - kind * LAG, 0)
+        d, h = tt // 2, tt % 2
+        s = 1 - 2 * side
+        src_z = z + s * d
+        valid = (t >= kind * LAG) & (t - kind * LAG < 2 * nz) & (src_z >= 0) & (src_z < nz)
+        valid = valid & jnp.logical_not((d == 0) & (side == 1))
+        src = jnp.clip(src_z, 0, nz - 1) * ny + jnp.where(kind == 0, y, 1 - y)
+        return valid, kind, d, h, s, src
+
+    zero = jnp.int32(0)
+    for h in range(2):
+        for cond, copy in sends(zero, zero, jnp.int32(h), jnp.int32(1), me):
+            pl.when(cond)(copy.start)
+    for copy in gcopies:
+        copy.wait()
+
+    def step(i, carry):
+        valid, kind, d, h, s, src = event(i)
+
+        @pl.when(valid)
+        def _():
+            @pl.when((d > 0) | (kind == 1))
+            def _():
+                pltpu.make_async_remote_copy(
+                    src_ref=lbuf.at[src, h],
+                    dst_ref=lbuf.at[src, h],
+                    send_sem=fwd_send.at[(src * 2 + h) * 3],
+                    recv_sem=fwd_recv.at[src * 2 + h],
+                    device_id=(pole, z * ny + 1 - y),
+                    device_id_type=MESH,
+                ).wait_recv()
+                for cond, copy in sends(kind, d, h, s, src):
+                    pl.when(cond)(copy.start)
+
+            cols = pl.ds(pl.multiple_of(src * rows + h * half, half), half)
+            g_r, g_i = gbuf[0, :, cols], gbuf[1, :, cols]
+            l_r, l_i = lbuf[src, h, 0], lbuf[src, h, 1]
+            acc[0] += dot(g_r, l_r) - dot(g_i, l_i)
+            acc[1] += dot(g_r, l_i) + dot(g_i, l_r)
+
+        return carry
+
+    lax.fori_loop(0, 4 * (2 * nz + LAG), step, 0)
+
+    w_r, w_i = weights[0, 0], weights[0, 1]
+    x_r, x_i = -acc[0], -acc[1]
+    dens = (w_r * x_i + w_i * x_r).astype(jnp.bfloat16)
+    other = (w_r * x_r - w_i * x_i).astype(jnp.bfloat16)
+
+    p_copies = []
+    for k in range(1, n_pole):
+        q = lax.rem(pole + k, n_pole)
+        packed[k] = dot(place[q], dens).astype(jnp.bfloat16)
+        p_copies.append(pltpu.make_async_remote_copy(
+            src_ref=packed.at[k], dst_ref=rbuf.at[k - 1],
+            send_sem=p_send.at[k - 1], recv_sem=p_recv.at[k - 1],
+            device_id=(q, me), device_id_type=MESH,
+        ))
+        p_copies[-1].start()
+
+    quad = jnp.zeros((qbuf.shape[2], qbuf.shape[2]), jnp.float32)
+    for h in range(2):
+        part = slice(h * half, (h + 1) * half)
+        quad += dot(lbuf[me, h, 0], dens[part], 0) + dot(lbuf[me, h, 1], other[part], 0)
+    term = w_r * diag[0, 1].astype(jnp.float32) + w_i * diag[0, 0].astype(jnp.float32)
+    for p in range(n_pole):
+        for g in range(n_grid):
+            at = (g * n_pole + p) * sub
+            qbuf[p, g * sub:(g + 1) * sub] = -quad[at:at + sub]
+        mine = pl.ds(pl.multiple_of(me * sub, sub), sub)
+        qbuf[p, mine] += term[p * sub:(p + 1) * sub]
+    a_copies = []
+    for k in range(1, n_pole):
+        q = lax.rem(pole + k, n_pole)
+        a_copies.append(pltpu.make_async_remote_copy(
+            src_ref=qbuf.at[q], dst_ref=abuf.at[k - 1],
+            send_sem=a_send.at[k - 1], recv_sem=a_recv.at[k - 1],
+            device_id=(q, me), device_id_type=MESH,
+        ))
+        a_copies[-1].start()
+
+    owned = dot(place[pole], dens)
+
+    total = qbuf[pole]
+    for k in range(1, n_pole):
+        a_copies[k - 1].wait_recv()
+        total += abuf[k - 1]
+    for g in range(n_grid):
+        sbuf[g] = total[g * sub:(g + 1) * sub]
+    b_copies = []
+    for k in range(1, n_grid):
+        g = lax.rem(me + k, n_grid)
+        b_copies.append(pltpu.make_async_remote_copy(
+            src_ref=sbuf.at[g], dst_ref=bbuf.at[k - 1],
+            send_sem=b_send.at[k - 1], recv_sem=b_recv.at[k - 1],
+            device_id=(pole, g), device_id_type=MESH,
+        ))
+        b_copies[-1].start()
+
+    for k in range(1, n_pole):
+        p_copies[k - 1].wait_recv()
+        owned += rbuf[k - 1].astype(jnp.float32)
+    patch_ref[...] = owned.astype(jnp.bfloat16)
+
+    final = sbuf[me]
+    for k in range(1, n_grid):
+        b_copies[k - 1].wait_recv()
+        final += bbuf[k - 1]
+    obuf[pole] = final
+    c_copies = []
+    for k in range(1, n_pole):
+        q = lax.rem(pole + k, n_pole)
+        c_copies.append(pltpu.make_async_remote_copy(
+            src_ref=obuf.at[pole], dst_ref=obuf.at[pole],
+            send_sem=c_send.at[k - 1], recv_sem=c_recv.at[k - 1],
+            device_id=(q, me), device_id_type=MESH,
+        ))
+        c_copies[-1].start()
+
+    def drain(i, carry):
+        valid, kind, d, h, s, src = event(i)
+        for cond, copy in sends(kind, d, h, s, src):
+            pl.when(valid & cond)(copy.wait_send)
+        return carry
+
+    lax.fori_loop(0, 4 * (2 * nz + LAG), drain, 0)
+    for copy in p_copies + a_copies + b_copies:
+        copy.wait_send()
+    for k in range(1, n_pole):
+        c_copies[k - 1].wait()
+    for p in range(n_pole):
+        dd_ref[p * sub:(p + 1) * sub] = obuf[p]
+
+
+def per_device(n_pole, n_grid, trailing, panel, diag_inverse, pole_weights, owner_map, ham_slab):
+    rows, m = trailing.shape[2:]
+    w = panel.shape[3]
+    half = rows // 2
+    cap = 2 * rows // n_pole
+    sub = w // n_grid // n_pole
+    vmem = pl.BlockSpec(memory_space=pltpu.VMEM)
+    dma = pltpu.SemaphoreType.DMA
+    patch, density_diag = pl.pallas_call(
+        functools.partial(kernel, n_pole, n_grid),
+        out_shape=(
+            jax.ShapeDtypeStruct((cap, w), jnp.bfloat16),
+            jax.ShapeDtypeStruct((w // n_grid, w), jnp.float32),
+        ),
+        in_specs=[
+            pl.BlockSpec(memory_space=pl.ANY),
+            pl.BlockSpec(memory_space=pl.ANY),
+            pl.BlockSpec(memory_space=pltpu.SMEM),
+            vmem,
+            vmem,
+        ],
+        out_specs=(vmem, vmem),
+        scratch_shapes=[
+            pltpu.VMEM((2, rows, m), jnp.bfloat16),
+            pltpu.VMEM((n_grid, 2, 2, half, w), jnp.bfloat16),
+            pltpu.VMEM((2, rows, w), jnp.float32),
+            pltpu.VMEM((n_pole, cap, rows), jnp.bfloat16),
+            pltpu.VMEM((n_pole, cap, w), jnp.bfloat16),
+            pltpu.VMEM((n_pole - 1, cap, w), jnp.bfloat16),
+            pltpu.VMEM((n_pole, n_grid * sub, w), jnp.float32),
+            pltpu.VMEM((n_pole - 1, n_grid * sub, w), jnp.float32),
+            pltpu.VMEM((n_grid, sub, w), jnp.float32),
+            pltpu.VMEM((n_grid - 1, sub, w), jnp.float32),
+            pltpu.VMEM((n_pole, sub, w), jnp.float32),
+            dma((2,)),
+            dma((4,)),
+            dma((n_grid * 6,)),
+            dma((n_grid * 2,)),
+            dma((n_pole - 1,)),
+            dma((n_pole - 1,)),
+            dma((n_pole - 1,)),
+            dma((n_pole - 1,)),
+            dma((n_grid - 1,)),
+            dma((n_grid - 1,)),
+            dma((n_pole - 1,)),
+            dma((n_pole - 1,)),
+        ],
+        compiler_params=pltpu.CompilerParams(
+            collective_id=0, has_side_effects=True, vmem_limit_bytes=40 * 1024 * 1024
+        ),
+        cost_estimate=pl.CostEstimate(
+            flops=8 * rows * m * w, bytes_accessed=4 * rows * m, transcendentals=0
+        ),
+    )(trailing, panel, pole_weights, owner_map.reshape(1, rows), diag_inverse)
+    patch_energy = jnp.dot(patch, ham_slab, preferred_element_type=jnp.float32).astype(jnp.bfloat16)
+    return (density_diag, patch_energy)
+
+
 def solution(mesh):
+    n_pole, n_grid = mesh.shape["pole"], mesh.shape["grid"]
     placed = (
         P("pole", None, "grid", None),
         P("pole", None, "grid", None),
@@ -68,8 +352,24 @@
         P("grid", None),
         P(),
     )
+
+    def body(trailing, panel, *rest):
+        rows, w = panel.shape[2:]
+        fits = (
+            panel.shape[0] == 1
+            and n_pole <= 16
+            and n_grid % 2 == 0
+            and rows % 256 == 0
+            and (2 * rows // n_pole) % 16 == 0
+            and w % (8 * n_grid * n_pole) == 0
+            and w % 128 == 0
+        )
+        if fits:
+            return per_device(n_pole, n_grid, trailing, panel, *rest)
+        return per_device_small(trailing, panel, *rest)
+
     return jax.shard_map(
-        per_device,
+        body,
         mesh=mesh,
         in_specs=placed,
         out_specs=(P("grid", None), P(("pole", "grid"), None)),

time: 218 us -> 81.6 us (0.37)
  waiting for transfers between devices: 165 us -> 0 us
  Pallas kernels: 0 us -> 71.4 us
  matrix products: 18.1 us -> 2.05 us
  between operations: 13.9 us -> 0.67 us
  blocking collectives: 11.5 us -> 0 us
  other arithmetic: 3.05 us -> 0 us
    all_gather x1 -> x0, waiting for transfers between devices: 74.3 us -> none  [per_device(): piece = lax.all_gather(panel, 'grid', axis=2, tiled=True)]
    pallas_call x0 -> x1, Pallas kernels: none -> 71.4 us  [per_device(): pl.pallas_call(functools.partial(kernel, n_pole, n_grid), out_shape=(jax....]
    unnamed x4 -> x0, waiting for transfers between devices: 61.6 us -> none
    psum x1 -> x0, waiting for transfers between devices: 29.5 us -> none  [per_device(): total_rows = lax.psum(density_rows, 'pole')]
    dot_general x9 -> x0, matrix products: 16.1 us -> none  [the longest x8 14.3 us: product(): return jnp.einsum(form, first, second, preferred_element_type=jnp.float32)]
    psum x1 -> x0, blocking collectives: 11.5 us -> none  [per_device(): density_diag = lax.psum(mine, 'pole')]
    unnamed x13, local copies, waits for them, and re-layouts: 3.62 us -> 7.28 us
  transfers between devices with their start and end apart: 3 -> 0, of which waited for: 3 -> 0; matrix products, arithmetic and copies ran while one was open for 5% -> 0% of each run, Pallas kernels for 0% -> 0%
where the time goes in v1:
time: 81.6 us; the launch traced here: 81.4 us
  Pallas kernels  71.4 us (88%)
  local copies, waits for them, and re-layouts  7.28 us (9%)
  matrix products  2.05 us (3%)
    pallas_call x1, Pallas kernels, per_device(): pl.pallas_call(functools.partial(kernel, n_pole, n_grid), out_shape=(jax....  71.4 us
    unnamed x13, local copies, waits for them, and re-layouts  7.28 us
    dot_general x1, matrix products, per_device(): jnp.dot(patch, ham_slab, preferred_element_type=jnp.float32)  2.05 us

profile of v1, /device:TPU:0, one launch (start us, length us, event | category | flops | bytes accessed | tf_op | source)
XLA Modules:
  0.0 81.4 jit_solution(1946692812397876679)
XLA Ops:
  0.6 0.0 copy-start
  0.6 0.0 copy-start.1
  0.7 3.5 %copy-done.1 = bf16[1,2,512,4096]{3,2,1,0:T(8,128)(2,1)S(1)} copy-done((bf16[1,2,512,4096]{3,2,1,0:T(8,128)(2,1)S(1)}, bf16[1,2,512,4096]{3,2,1,0:T(8,128)(2,1)}, u32[]{:S(2)}) %copy-start.1) | copy-done | bytes 8388632
  4.2 0.0 copy-start.2
  4.2 1.0 %copy-done.2 = bf16[1,2,512,256]{3,2,1,0:T(8,128)(2,1)S(1)} copy-done((bf16[1,2,512,256]{3,2,1,0:T(8,128)(2,1)S(1)}, bf16[1,2,512,256]{3,2,1,0:T(8,128)(2,1)}, u32[]{:S(2)}) %copy-start.2) | copy-done | bytes 524312
  5.2 0.0 copy-start.3
  5.2 0.8 copy-done.3
  6.0 0.0 copy-start.4
  6.0 0.7 copy-done.4
  6.7 0.0 copy-start.5
  6.7 0.7 copy-done.5
  7.3 71.4 %shard_map.77 = (bf16[256,256]{1,0:T(8,128)(2,1)S(1)}, f32[32,256]{1,0:T(8,128)S(1)}) custom-call(bf16[1,2,512,4096]{3,2,1,0:T(8,128)(2,1)S(1)} %copy-done.1, bf16[1,2,512,256]{3,2,1,0:T(8,128)(2,1)S(1)} %copy-done.2, f32[1,2]{1,0:T(1,128)S(1)} %copy-done.5, s32[1,512]{1,0:T(1,128)S(1)} %bitcast.3, bf16[1,2,32,256]{3,2,1,0:T(8,128)(2,1)S(1)} %copy-done.3), custom_call_target="tpu_custom_call" | custom-call | flops 4294967296 | bytes 8388608 | tf_op jit(solution)/shard_map/pallas_call | solution.py:295
  78.7 0.0 copy-done
  78.7 2.0 %convolution_convert_fusion = bf16[256,4096]{1,0:T(8,128)(2,1)} fusion(bf16[256,256]{1,0:T(8,128)(2,1)S(1)} %get-tuple-element.5, bf16[256,4096]{1,0:T(8,128)(2,1)S(1)} %copy-done), kind=kOutput, calls=%fused_computation | convolution fusion | flops 537919488 | bytes 4325376 | tf_op jit(solution)/shard_map/dot_general | solution.py:341
  80.8 0.6 copy.9
Async XLA Ops:
  0.6 78.1 %copy-start = (bf16[256,4096]{1,0:T(8,128)(2,1)S(1)}, bf16[256,4096]{1,0:T(8,128)(2,1)}, u32[]{:S(2)}) copy-start(bf16[256,4096]{1,0:T(8,128)(2,1)} %param.11) | copy-start | bytes 6291460
  0.6 3.5 %copy-start.1 = (bf16[1,2,512,4096]{3,2,1,0:T(8,128)(2,1)S(1)}, bf16[1,2,512,4096]{3,2,1,0:T(8,128)(2,1)}, u32[]{:S(2)}) copy-start(bf16[1,2,512,4096]{3,2,1,0:T(8,128)(2,1)} %trailing.1) | copy-start | bytes 25165828
  4.2 1.0 %copy-start.2 = (bf16[1,2,512,256]{3,2,1,0:T(8,128)(2,1)S(1)}, bf16[1,2,512,256]{3,2,1,0:T(8,128)(2,1)}, u32[]{:S(2)}) copy-start(bf16[1,2,512,256]{3,2,1,0:T(8,128)(2,1)} %panel.1) | copy-start | bytes 1572868
  5.2 0.8 copy-start.3
  6.0 0.7 copy-start.4
  6.7 0.7 copy-start.5

commit v2 on v1

--- a/solution.py
+++ b/solution.py
@@ -74,15 +74,15 @@
 
 def kernel(
     n_pole, n_grid, trailing, panel, weights, owners, diag, patch_ref, dd_ref,
-    gbuf, lbuf, acc, place, packed, rbuf, qbuf, abuf, sbuf, bbuf, obuf,
-    gsem, lsem, fwd_send, fwd_recv, p_send, p_recv, a_send, a_recv, b_send, b_recv, c_send, c_recv,
+    gbuf, lbuf, acc, place, packed, mbuf, sums, pbuf, rbuf, qbuf, abuf, bbuf, obuf,
+    gsem, lsem, fwd_send, fwd_recv, m_sem, p_send, p_recv, a_send, a_recv, c_send, c_recv,
 ):
     ny = 2
     nz = n_grid // ny
     rows = gbuf.shape[1]
     half = rows // 2
     cap = rbuf.shape[1]
-    sub = obuf.shape[1]
+    sub, w = obuf.shape[1:]
     pole, me = lax.axis_index("pole"), lax.axis_index("grid")
     z, y = me // ny, me % ny
 
@@ -199,73 +199,60 @@
     dens = (w_r * x_i + w_i * x_r).astype(jnp.bfloat16)
     other = (w_r * x_r - w_i * x_i).astype(jnp.bfloat16)
 
-    p_copies = []
-    for k in range(1, n_pole):
-        q = lax.rem(pole + k, n_pole)
-        packed[k] = dot(place[q], dens).astype(jnp.bfloat16)
-        p_copies.append(pltpu.make_async_remote_copy(
-            src_ref=packed.at[k], dst_ref=rbuf.at[k - 1],
-            send_sem=p_send.at[k - 1], recv_sem=p_recv.at[k - 1],
-            device_id=(q, me), device_id_type=MESH,
-        ))
-        p_copies[-1].start()
-
-    quad = jnp.zeros((qbuf.shape[2], qbuf.shape[2]), jnp.float32)
+    core, cap_sets = pole % 2, n_pole // 2
+    mate = pole + 1 - 2 * core
+    for j in range(cap_sets):
+        packed[j] = dot(place[2 * j + 1 - core], dens).astype(jnp.bfloat16)
+    mate_copy = pltpu.make_async_remote_copy(
+        src_ref=packed, dst_ref=mbuf, send_sem=m_sem.at[0], recv_sem=m_sem.at[1],
+        device_id=(mate, me), device_id_type=MESH,
+    )
+    mate_copy.start()
+
+    quad = jnp.zeros((w, w), jnp.float32)
     for h in range(2):
         part = slice(h * half, (h + 1) * half)
         quad += dot(lbuf[me, h, 0], dens[part], 0) + dot(lbuf[me, h, 1], other[part], 0)
-    term = w_r * diag[0, 1].astype(jnp.float32) + w_i * diag[0, 0].astype(jnp.float32)
-    for p in range(n_pole):
-        for g in range(n_grid):
-            at = (g * n_pole + p) * sub
-            qbuf[p, g * sub:(g + 1) * sub] = -quad[at:at + sub]
-        mine = pl.ds(pl.multiple_of(me * sub, sub), sub)
-        qbuf[p, mine] += term[p * sub:(p + 1) * sub]
+    qbuf[...] = -quad
+    for g in range(n_grid):
+        abuf[g] = qbuf[g * sub:(g + 1) * sub].astype(jnp.bfloat16)
     a_copies = []
-    for k in range(1, n_pole):
-        q = lax.rem(pole + k, n_pole)
+    for k in range(1, n_grid):
+        g = lax.rem(me + k, n_grid)
         a_copies.append(pltpu.make_async_remote_copy(
-            src_ref=qbuf.at[q], dst_ref=abuf.at[k - 1],
+            src_ref=abuf.at[g], dst_ref=bbuf.at[k - 1],
             send_sem=a_send.at[k - 1], recv_sem=a_recv.at[k - 1],
-            device_id=(q, me), device_id_type=MESH,
+            device_id=(pole, g), device_id_type=MESH,
         ))
         a_copies[-1].start()
-
-    owned = dot(place[pole], dens)
-
-    total = qbuf[pole]
-    for k in range(1, n_pole):
+    term = w_r * diag[0, 1].astype(jnp.float32) + w_i * diag[0, 0].astype(jnp.float32)
+    final = term + qbuf[pl.ds(pl.multiple_of(me * sub, sub), sub)]
+    for j in range(cap_sets):
+        sums[j] = dot(place[2 * j + core], dens)
+
+    mate_copy.wait_recv()
+    p_copies = []
+    for k in range(1, cap_sets):
+        j = lax.rem(pole // 2 + k, cap_sets)
+        pbuf[k - 1] = (sums[j] + mbuf[j].astype(jnp.float32)).astype(jnp.bfloat16)
+        p_copies.append(pltpu.make_async_remote_copy(
+            src_ref=pbuf.at[k - 1], dst_ref=rbuf.at[k - 1],
+            send_sem=p_send.at[k - 1], recv_sem=p_recv.at[k - 1],
+            device_id=(2 * j + core, me), device_id_type=MESH,
+        ))
+        p_copies[-1].start()
+    owned = sums[pole // 2] + mbuf[pole // 2].astype(jnp.float32)
+
+    for k in range(1, n_grid):
         a_copies[k - 1].wait_recv()
-        total += abuf[k - 1]
-    for g in range(n_grid):
-        sbuf[g] = total[g * sub:(g + 1) * sub]
-    b_copies = []
-    for k in range(1, n_grid):
-        g = lax.rem(me + k, n_grid)
-        b_copies.append(pltpu.make_async_remote_copy(
-            src_ref=sbuf.at[g], dst_ref=bbuf.at[k - 1],
-            send_sem=b_send.at[k - 1], recv_sem=b_recv.at[k - 1],
-            device_id=(pole, g), device_id_type=MESH,
-        ))
-        b_copies[-1].start()
-
-    for k in range(1, n_pole):
-        p_copies[k - 1].wait_recv()
-        owned += rbuf[k - 1].astype(jnp.float32)
-    patch_ref[...] = owned.astype(jnp.bfloat16)
-
-    final = sbuf[me]
-    for k in range(1, n_grid):
-        b_copies[k - 1].wait_recv()
-        final += bbuf[k - 1]
+        final += bbuf[k - 1].astype(jnp.float32)
     obuf[pole] = final
     c_copies = []
     for k in range(1, n_pole):
-        q = lax.rem(pole + k, n_pole)
         c_copies.append(pltpu.make_async_remote_copy(
             src_ref=obuf.at[pole], dst_ref=obuf.at[pole],
             send_sem=c_send.at[k - 1], recv_sem=c_recv.at[k - 1],
-            device_id=(q, me), device_id_type=MESH,
+            device_id=(lax.rem(pole + k, n_pole), me), device_id_type=MESH,
         ))
         c_copies[-1].start()
 
@@ -276,12 +263,20 @@
         return carry
 
     lax.fori_loop(0, 4 * (2 * nz + LAG), drain, 0)
-    for copy in p_copies + a_copies + b_copies:
+    mate_copy.wait_send()
+    for copy in p_copies:
+        copy.wait()
+    for k in range(1, cap_sets):
+        owned += rbuf[k - 1].astype(jnp.float32)
+    patch_ref[...] = owned.astype(jnp.bfloat16)
+    for copy in a_copies:
         copy.wait_send()
     for k in range(1, n_pole):
         c_copies[k - 1].wait()
-    for p in range(n_pole):
-        dd_ref[p * sub:(p + 1) * sub] = obuf[p]
+    result = obuf[0]
+    for p in range(1, n_pole):
+        result += obuf[p]
+    dd_ref[...] = result
 
 
 def per_device(n_pole, n_grid, trailing, panel, diag_inverse, pole_weights, owner_map, ham_slab):
@@ -289,7 +284,7 @@
     w = panel.shape[3]
     half = rows // 2
     cap = 2 * rows // n_pole
-    sub = w // n_grid // n_pole
+    sub = w // n_grid
     vmem = pl.BlockSpec(memory_space=pltpu.VMEM)
     dma = pltpu.SemaphoreType.DMA
     patch, density_diag = pl.pallas_call(
@@ -311,28 +306,29 @@
             pltpu.VMEM((n_grid, 2, 2, half, w), jnp.bfloat16),
             pltpu.VMEM((2, rows, w), jnp.float32),
             pltpu.VMEM((n_pole, cap, rows), jnp.bfloat16),
-            pltpu.VMEM((n_pole, cap, w), jnp.bfloat16),
-            pltpu.VMEM((n_pole - 1, cap, w), jnp.bfloat16),
-            pltpu.VMEM((n_pole, n_grid * sub, w), jnp.float32),
-            pltpu.VMEM((n_pole - 1, n_grid * sub, w), jnp.float32),
-            pltpu.VMEM((n_grid, sub, w), jnp.float32),
-            pltpu.VMEM((n_grid - 1, sub, w), jnp.float32),
+            pltpu.VMEM((n_pole // 2, cap, w), jnp.bfloat16),
+            pltpu.VMEM((n_pole // 2, cap, w), jnp.bfloat16),
+            pltpu.VMEM((n_pole // 2, cap, w), jnp.float32),
+            pltpu.VMEM((n_pole // 2 - 1, cap, w), jnp.bfloat16),
+            pltpu.VMEM((n_pole // 2 - 1, cap, w), jnp.bfloat16),
+            pltpu.VMEM((w, w), jnp.float32),
+            pltpu.VMEM((n_grid, sub, w), jnp.bfloat16),
+            pltpu.VMEM((n_grid - 1, sub, w), jnp.bfloat16),
             pltpu.VMEM((n_pole, sub, w), jnp.float32),
             dma((2,)),
             dma((4,)),
             dma((n_grid * 6,)),
             dma((n_grid * 2,)),
-            dma((n_pole - 1,)),
-            dma((n_pole - 1,)),
-            dma((n_pole - 1,)),
-            dma((n_pole - 1,)),
+            dma((2,)),
+            dma((n_pole // 2 - 1,)),
+            dma((n_pole // 2 - 1,)),
             dma((n_grid - 1,)),
             dma((n_grid - 1,)),
             dma((n_pole - 1,)),
             dma((n_pole - 1,)),
         ],
         compiler_params=pltpu.CompilerParams(
-            collective_id=0, has_side_effects=True, vmem_limit_bytes=40 * 1024 * 1024
+            collective_id=0, has_side_effects=True, vmem_limit_bytes=60 * 1024 * 1024
         ),
         cost_estimate=pl.CostEstimate(
             flops=8 * rows * m * w, bytes_accessed=4 * rows * m, transcendentals=0
@@ -357,11 +353,12 @@
         rows, w = panel.shape[2:]
         fits = (
             panel.shape[0] == 1
-            and n_pole <= 16
+            and n_pole % 2 == 0
+            and 4 <= n_pole <= 16
             and n_grid % 2 == 0
             and rows % 256 == 0
             and (2 * rows // n_pole) % 16 == 0
-            and w % (8 * n_grid * n_pole) == 0
+            and w % (16 * n_grid) == 0
             and w % 128 == 0
         )
         if fits:

time: 81.6 us -> 68.9 us (0.84)
  Pallas kernels: 71.4 us -> 64.5 us
  local copies, waits for them, and re-layouts: 7.28 us -> 0.63 us
  matrix products: 2.05 us -> 2.94 us
    pallas_call x1, Pallas kernels: 71.4 us -> 64.5 us  [per_device(): pl.pallas_call(functools.partial(kernel, n_pole, n_grid), out_shape=(jax....]
    unnamed x13 -> x5, local copies, waits for them, and re-layouts: 7.28 us -> 0.63 us
    dot_general x1, matrix products: 2.05 us -> 2.94 us  [per_device(): jnp.dot(patch, ham_slab, preferred_element_type=jnp.float32)]
where the time goes in v2:
time: 68.9 us; the launch traced here: 68.8 us
  Pallas kernels  64.5 us (94%)
  matrix products  2.94 us (4%)
    pallas_call x1, Pallas kernels, per_device(): pl.pallas_call(functools.partial(kernel, n_pole, n_grid), out_shape=(jax....  64.5 us
    dot_general x1, matrix products, per_device(): jnp.dot(patch, ham_slab, preferred_element_type=jnp.float32)  2.94 us

profile of v2, /device:TPU:0, one launch (start us, length us, event | category | flops | bytes accessed | tf_op | source)
XLA Modules:
  0.0 68.8 jit_solution(13418069553668449529)
XLA Ops:
  0.6 0.0 copy-start
  0.6 64.5 %shard_map.77 = (bf16[256,256]{1,0:T(8,128)(2,1)}, f32[32,256]{1,0:T(8,128)}) custom-call(bf16[1,2,512,4096]{3,2,1,0:T(8,128)(2,1)} %trailing.1, bf16[1,2,512,256]{3,2,1,0:T(8,128)(2,1)} %panel.1, f32[1,2]{1,0:T(1,128)} %weights.1, s32[1,512]{1,0:T(1,128)} %bitcast.3, bf16[1,2,32,256]{3,2,1,0:T(8,128)(2,1)} %diag.1), custom_call_target="tpu_custom_call" | custom-call | flops 4294967296 | bytes 8388608 | tf_op jit(solution)/shard_map/pallas_call | solution.py:290
  65.2 0.0 copy-done
  65.2 0.0 copy-start.1
  65.2 2.9 %convolution_convert_fusion = bf16[256,4096]{1,0:T(8,128)(2,1)} fusion(bf16[256,256]{1,0:T(8,128)(2,1)} %get-tuple-element.5, bf16[256,4096]{1,0:T(8,128)(2,1)S(1)} %copy-done), kind=kOutput, calls=%fused_computation | convolution fusion | flops 537919488 | bytes 4325376 | tf_op jit(solution)/shard_map/dot_general | solution.py:337
  68.2 0.0 copy-done.1
  68.2 0.6 copy.9
Async XLA Ops:
  0.6 64.6 %copy-start = (bf16[256,4096]{1,0:T(8,128)(2,1)S(1)}, bf16[256,4096]{1,0:T(8,128)(2,1)}, u32[]{:S(2)}) copy-start(bf16[256,4096]{1,0:T(8,128)(2,1)} %param.11) | copy-start | bytes 6291460
  65.2 3.0 %copy-start.1 = (f32[32,256]{1,0:T(8,128)S(1)}, f32[32,256]{1,0:T(8,128)}, u32[]{:S(2)}) copy-start(f32[32,256]{1,0:T(8,128)} %get-tuple-element.8) | copy-start | bytes 98308

commit v3 on v2

--- a/solution.py
+++ b/solution.py
@@ -130,10 +130,14 @@
     def sends(kind, d, h, s, src):
         own_line = kind == 0
         first = d == 0
-        turn = (kind == 1) & first & (h == 0)
-        up = (z + 1 < nz) & ((own_line & (first | (s == -1))) | turn)
-        down = (z >= 1) & ((own_line & (first | (s == 1))) | turn)
-        over = own_line & jnp.logical_not((d == 1) & (h == 0))
+        src_z = src // ny
+        turn = (kind == 1) & (h == 0)
+        turn_up = turn & jnp.where(z + 1 == nz - 1, src_z == 0, first)
+        turn_down = turn & jnp.where(z == 1, src_z == nz - 1, first)
+        up = (z + 1 < nz) & ((own_line & (first | (s == -1))) | turn_up)
+        down = (z >= 1) & ((own_line & (first | (s == 1))) | turn_down)
+        spared = jnp.where((z == 0) | (z == nz - 1), nz - 1, 1)
+        over = own_line & jnp.logical_not((d == spared) & (h == 0))
         targets = (jnp.minimum(z + 1, nz - 1) * ny + y, jnp.maximum(z - 1, 0) * ny + y, z * ny + 1 - y)
         out = []
         for j, (cond, target) in enumerate(zip((up, down, over), targets)):
@@ -355,6 +359,7 @@
             panel.shape[0] == 1
             and n_pole % 2 == 0
             and 4 <= n_pole <= 16
+            and n_grid >= 4
             and n_grid % 2 == 0
             and rows % 256 == 0
             and (2 * rows // n_pole) % 16 == 0

time: 68.9 us -> 64.8 us (0.940)
  Pallas kernels: 64.5 us -> 60.4 us
    pallas_call x1, Pallas kernels: 64.5 us -> 60.4 us  [per_device(): pl.pallas_call(functools.partial(kernel, n_pole, n_grid), out_shape=(jax....]
where the time goes in v3:
time: 64.8 us; the launch traced here: 64.6 us
  Pallas kernels  60.4 us (93%)
  matrix products  2.94 us (5%)
  between operations  0.66 us (1%)
    pallas_call x1, Pallas kernels, per_device(): pl.pallas_call(functools.partial(kernel, n_pole, n_grid), out_shape=(jax....  60.4 us
    dot_general x1, matrix products, per_device(): jnp.dot(patch, ham_slab, preferred_element_type=jnp.float32)  2.94 us

profile of v3, /device:TPU:0, one launch (start us, length us, event | category | flops | bytes accessed | tf_op | source)
XLA Modules:
  0.0 64.6 jit_solution(17737910570671157389)
XLA Ops:
  0.6 0.0 copy-start
  0.6 60.4 %shard_map.77 = (bf16[256,256]{1,0:T(8,128)(2,1)}, f32[32,256]{1,0:T(8,128)}) custom-call(bf16[1,2,512,4096]{3,2,1,0:T(8,128)(2,1)} %trailing.1, bf16[1,2,512,256]{3,2,1,0:T(8,128)(2,1)} %panel.1, f32[1,2]{1,0:T(1,128)} %weights.1, s32[1,512]{1,0:T(1,128)} %bitcast.3, bf16[1,2,32,256]{3,2,1,0:T(8,128)(2,1)} %diag.1), custom_call_target="tpu_custom_call" | custom-call | flops 4294967296 | bytes 8388608 | tf_op jit(solution)/shard_map/pallas_call | solution.py:294
  61.0 0.0 copy-done
  61.0 0.0 copy-start.1
  61.0 2.9 %convolution_convert_fusion = bf16[256,4096]{1,0:T(8,128)(2,1)} fusion(bf16[256,256]{1,0:T(8,128)(2,1)} %get-tuple-element.5, bf16[256,4096]{1,0:T(8,128)(2,1)S(1)} %copy-done), kind=kOutput, calls=%fused_computation | convolution fusion | flops 537919488 | bytes 4325376 | tf_op jit(solution)/shard_map/dot_general | solution.py:341
  64.0 0.0 copy-done.1
  64.0 0.6 copy.9
Async XLA Ops:
  0.6 60.4 %copy-start = (bf16[256,4096]{1,0:T(8,128)(2,1)S(1)}, bf16[256,4096]{1,0:T(8,128)(2,1)}, u32[]{:S(2)}) copy-start(bf16[256,4096]{1,0:T(8,128)(2,1)} %param.11) | copy-start | bytes 6291460
  61.0 3.0 %copy-start.1 = (f32[32,256]{1,0:T(8,128)S(1)}, f32[32,256]{1,0:T(8,128)}, u32[]{:S(2)}) copy-start(f32[32,256]{1,0:T(8,128)} %get-tuple-element.8) | copy-start | bytes 98308

commit v4 on v3

--- a/solution.py
+++ b/solution.py
@@ -8,7 +8,8 @@
 from jax.sharding import PartitionSpec as P
 
 MESH = pl.DeviceIdType.MESH
-LAG = 2
+LAG = 4
+CUTS = 4
 
 
 def complex_product(left_real, left_imag, right_real, right_imag, form):
@@ -80,7 +81,7 @@
     ny = 2
     nz = n_grid // ny
     rows = gbuf.shape[1]
-    half = rows // 2
+    half = rows // CUTS
     cap = rbuf.shape[1]
     sub, w = obuf.shape[1:]
     pole, me = lax.axis_index("pole"), lax.axis_index("grid")
@@ -93,7 +94,7 @@
         pltpu.make_async_copy(
             panel.at[0, c, pl.ds(h * half, half)], lbuf.at[me, h, c], lsem.at[2 * h + c]
         )
-        for h in range(2)
+        for h in range(CUTS)
         for c in range(2)
     ]
     for copy in lcopies + gcopies:
@@ -131,21 +132,21 @@
         own_line = kind == 0
         first = d == 0
         src_z = src // ny
-        turn = (kind == 1) & (h == 0)
+        turn = (kind == 1) & (h < CUTS // 2)
         turn_up = turn & jnp.where(z + 1 == nz - 1, src_z == 0, first)
         turn_down = turn & jnp.where(z == 1, src_z == nz - 1, first)
         up = (z + 1 < nz) & ((own_line & (first | (s == -1))) | turn_up)
         down = (z >= 1) & ((own_line & (first | (s == 1))) | turn_down)
         spared = jnp.where((z == 0) | (z == nz - 1), nz - 1, 1)
-        over = own_line & jnp.logical_not((d == spared) & (h == 0))
+        over = own_line & jnp.logical_not((d == spared) & (h < CUTS // 2))
         targets = (jnp.minimum(z + 1, nz - 1) * ny + y, jnp.maximum(z - 1, 0) * ny + y, z * ny + 1 - y)
         out = []
         for j, (cond, target) in enumerate(zip((up, down, over), targets)):
             out.append((cond, pltpu.make_async_remote_copy(
                 src_ref=lbuf.at[src, h],
                 dst_ref=lbuf.at[src, h],
-                send_sem=fwd_send.at[(src * 2 + h) * 3 + j],
-                recv_sem=fwd_recv.at[src * 2 + h],
+                send_sem=fwd_send.at[(src * CUTS + h) * 3 + j],
+                recv_sem=fwd_recv.at[src * CUTS + h],
                 device_id=(pole, target),
                 device_id_type=MESH,
             )))
@@ -155,16 +156,16 @@
         t, r = i // 4, i % 4
         kind, side = r // 2, r % 2
         tt = jnp.maximum(t - kind * LAG, 0)
-        d, h = tt // 2, tt % 2
+        d, h = tt // CUTS, tt % CUTS
         s = 1 - 2 * side
         src_z = z + s * d
-        valid = (t >= kind * LAG) & (t - kind * LAG < 2 * nz) & (src_z >= 0) & (src_z < nz)
+        valid = (t >= kind * LAG) & (t - kind * LAG < CUTS * nz) & (src_z >= 0) & (src_z < nz)
         valid = valid & jnp.logical_not((d == 0) & (side == 1))
         src = jnp.clip(src_z, 0, nz - 1) * ny + jnp.where(kind == 0, y, 1 - y)
         return valid, kind, d, h, s, src
 
     zero = jnp.int32(0)
-    for h in range(2):
+    for h in range(CUTS):
         for cond, copy in sends(zero, zero, jnp.int32(h), jnp.int32(1), me):
             pl.when(cond)(copy.start)
     for copy in gcopies:
@@ -180,8 +181,8 @@
                 pltpu.make_async_remote_copy(
                     src_ref=lbuf.at[src, h],
                     dst_ref=lbuf.at[src, h],
-                    send_sem=fwd_send.at[(src * 2 + h) * 3],
-                    recv_sem=fwd_recv.at[src * 2 + h],
+                    send_sem=fwd_send.at[(src * CUTS + h) * 3],
+                    recv_sem=fwd_recv.at[src * CUTS + h],
                     device_id=(pole, z * ny + 1 - y),
                     device_id_type=MESH,
                 ).wait_recv()
@@ -196,7 +197,7 @@
 
         return carry
 
-    lax.fori_loop(0, 4 * (2 * nz + LAG), step, 0)
+    lax.fori_loop(0, 4 * (CUTS * nz + LAG), step, 0)
 
     w_r, w_i = weights[0, 0], weights[0, 1]
     x_r, x_i = -acc[0], -acc[1]
@@ -214,7 +215,7 @@
     mate_copy.start()
 
     quad = jnp.zeros((w, w), jnp.float32)
-    for h in range(2):
+    for h in range(CUTS):
         part = slice(h * half, (h + 1) * half)
         quad += dot(lbuf[me, h, 0], dens[part], 0) + dot(lbuf[me, h, 1], other[part], 0)
     qbuf[...] = -quad
@@ -266,7 +267,7 @@
             pl.when(valid & cond)(copy.wait_send)
         return carry
 
-    lax.fori_loop(0, 4 * (2 * nz + LAG), drain, 0)
+    lax.fori_loop(0, 4 * (CUTS * nz + LAG), drain, 0)
     mate_copy.wait_send()
     for copy in p_copies:
         copy.wait()
@@ -286,7 +287,7 @@
 def per_device(n_pole, n_grid, trailing, panel, diag_inverse, pole_weights, owner_map, ham_slab):
     rows, m = trailing.shape[2:]
     w = panel.shape[3]
-    half = rows // 2
+    half = rows // CUTS
     cap = 2 * rows // n_pole
     sub = w // n_grid
     vmem = pl.BlockSpec(memory_space=pltpu.VMEM)
@@ -307,7 +308,7 @@
         out_specs=(vmem, vmem),
         scratch_shapes=[
             pltpu.VMEM((2, rows, m), jnp.bfloat16),
-            pltpu.VMEM((n_grid, 2, 2, half, w), jnp.bfloat16),
+            pltpu.VMEM((n_grid, CUTS, 2, half, w), jnp.bfloat16),
             pltpu.VMEM((2, rows, w), jnp.float32),
             pltpu.VMEM((n_pole, cap, rows), jnp.bfloat16),
             pltpu.VMEM((n_pole // 2, cap, w), jnp.bfloat16),
@@ -320,9 +321,9 @@
             pltpu.VMEM((n_grid - 1, sub, w), jnp.bfloat16),
             pltpu.VMEM((n_pole, sub, w), jnp.float32),
             dma((2,)),
-            dma((4,)),
-            dma((n_grid * 6,)),
-            dma((n_grid * 2,)),
+            dma((2 * CUTS,)),
+            dma((n_grid * CUTS * 3,)),
+            dma((n_grid * CUTS,)),
             dma((2,)),
             dma((n_pole // 2 - 1,)),
             dma((n_pole // 2 - 1,)),
@@ -361,7 +362,7 @@
             and 4 <= n_pole <= 16
             and n_grid >= 4
             and n_grid % 2 == 0
-            and rows % 256 == 0
+            and rows % (128 * CUTS) == 0
             and (2 * rows // n_pole) % 16 == 0
             and w % (16 * n_grid) == 0
             and w % 128 == 0

time: 64.8 us -> 66 us (1.019)
  Pallas kernels: 60.4 us -> 61.6 us
    pallas_call x1, Pallas kernels: 60.4 us -> 61.6 us  [per_device(): pl.pallas_call(functools.partial(kernel, n_pole, n_grid), out_shape=(jax....]
where the time goes in v4:
time: 66 us; the launch traced here: 65.9 us
  Pallas kernels  61.6 us (93%)
  matrix products  2.94 us (4%)
  between operations  0.66 us (1%)
    pallas_call x1, Pallas kernels, per_device(): pl.pallas_call(functools.partial(kernel, n_pole, n_grid), out_shape=(jax....  61.6 us
    dot_general x1, matrix products, per_device(): jnp.dot(patch, ham_slab, preferred_element_type=jnp.float32)  2.94 us

profile of v4, /device:TPU:0, one launch (start us, length us, event | category | flops | bytes accessed | tf_op | source)
XLA Modules:
  0.0 65.9 jit_solution(5582136837502288369)
XLA Ops:
  0.6 0.0 copy-start
  0.6 61.6 %shard_map.77 = (bf16[256,256]{1,0:T(8,128)(2,1)}, f32[32,256]{1,0:T(8,128)}) custom-call(bf16[1,2,512,4096]{3,2,1,0:T(8,128)(2,1)} %trailing.1, bf16[1,2,512,256]{3,2,1,0:T(8,128)(2,1)} %panel.1, f32[1,2]{1,0:T(1,128)} %weights.1, s32[1,512]{1,0:T(1,128)} %bitcast.3, bf16[1,2,32,256]{3,2,1,0:T(8,128)(2,1)} %diag.1), custom_call_target="tpu_custom_call" | custom-call | flops 4294967296 | bytes 8388608 | tf_op jit(solution)/shard_map/pallas_call | solution.py:295
  62.3 0.0 copy-done
  62.3 0.0 copy-start.1
  62.3 2.9 %convolution_convert_fusion = bf16[256,4096]{1,0:T(8,128)(2,1)} fusion(bf16[256,256]{1,0:T(8,128)(2,1)} %get-tuple-element.5, bf16[256,4096]{1,0:T(8,128)(2,1)S(1)} %copy-done), kind=kOutput, calls=%fused_computation | convolution fusion | flops 537919488 | bytes 4325376 | tf_op jit(solution)/shard_map/dot_general | solution.py:342
  65.3 0.0 copy-done.1
  65.3 0.6 copy.9
Async XLA Ops:
  0.6 61.7 %copy-start = (bf16[256,4096]{1,0:T(8,128)(2,1)S(1)}, bf16[256,4096]{1,0:T(8,128)(2,1)}, u32[]{:S(2)}) copy-start(bf16[256,4096]{1,0:T(8,128)(2,1)} %param.11) | copy-start | bytes 6291460
  62.3 3.0 %copy-start.1 = (f32[32,256]{1,0:T(8,128)S(1)}, f32[32,256]{1,0:T(8,128)}, u32[]{:S(2)}) copy-start(f32[32,256]{1,0:T(8,128)} %get-tuple-element.8) | copy-start | bytes 98308
